TPU v7x, 512 devices: a whole 4x8x8 slice. The times are simulated.
512 devices in a mesh: tm: 16 (over z, core), space: 32 (over x, y).
Axes of the slice: x: 4, y: 8, z: 8, core: 2. Of those that a mesh axis runs over, the one named last changes fastest.
Arguments:
- queries: bfloat16 [16, 4096, 1120], P('tm', 'space'), may hold values from -6 to 6
- keys_in: bfloat16 [16, 4096, 1120], P('tm', 'space'), may hold values from -30 to 30
- values_in: bfloat16 [16, 4096, 1120], P('tm', 'space'), may hold values from -10 to 10
- grad_attn: bfloat16 [16, 4096, 1120], P('tm', 'space'), may hold values from -6 to 6
Outputs:
- mixed: bfloat16 [16, 4096, 1120], P('tm', 'space')
- grad_queries: bfloat16 [16, 4096, 1120], P('tm', 'space')
- grad_keys: bfloat16 [16, 4096, 1120], P('tm', 'space')
- values_gradient: bfloat16 [16, 4096, 1120], P('tm', 'space')
All inputs are finite; a program needn't handle non-finite values.
Results may differ from a plain program's by a relative error of at most 0.001.
Values sent between devices are 32-bit elements; how exact they have to be, the bound alone decides.
No kernel may reach another device: no remote copies, remote signals or barrier semaphores. Data moves between devices by JAX's collectives and lax.ppermute only.
A program may use at most 64 MiB of HBM per device.

v0:
```python
import math
import jax
import jax.numpy as jnp
from jax import lax
from jax.sharding import PartitionSpec as P

HEAD_DIM = 112
HIGH_PRECISION = lax.Precision.HIGHEST


def split_up(shard, dim, size):
    lengths = shard.shape
    pieces = shard.reshape(*lengths[:dim], size, lengths[dim] // size, *lengths[dim + 1 :])
    return jnp.moveaxis(pieces, dim, 0)


def sent_and_summed(shard, axis, dim):
    size = lax.axis_size(axis)
    pieces = lax.all_to_all(split_up(shard, dim, size), axis, 0, 0, tiled=True)
    return jnp.sum(pieces, axis=0)


def in_one_piece(arrays, axis, dim, along):
    widths = [math.prod(a.shape[along:]) for a in arrays]
    both = jnp.concatenate(
        [a.reshape(*a.shape[:along], w) for a, w in zip(arrays, widths)], axis=along
    )
    filled = sent_and_summed(both, axis, dim)
    pieces = jnp.split(filled, [sum(widths[:k]) for k in range(1, len(widths))], axis=along)
    return tuple(
        (b.reshape(*filled.shape[:along], *a.shape[along:]) for a, b in zip(arrays, pieces))
    )


def sent_to_all(shard, axis):
    size = lax.axis_size(axis)
    return lax.all_to_all(
        jnp.broadcast_to(shard[None], (size, *shard.shape)), axis, 0, 0, tiled=True
    )


def collected_together(shard, axis):
    leaves = jax.tree.leaves(shard)
    order = sorted(range(len(leaves)), key=lambda k: -leaves[k].size)
    width = (1, *leaves[order[0]].shape)[-1]
    lines = [
        jnp.pad(leaves[k].reshape(-1), (0, -leaves[k].size % width)).reshape(-1, width)
        for k in order
    ]
    both, at, found = (sent_to_all(jnp.concatenate(lines), axis), 0, {})
    for k, line in zip(order, lines):
        share = both[:, at : at + len(line)].reshape(len(both), -1)
        found[k] = share[:, : leaves[k].size].reshape(-1, *leaves[k].shape)
        at += len(line)
    numbers = iter(range(len(leaves)))
    return jax.tree.map(lambda _: found[next(numbers)], shard)


def folded_in_pairs(pieces, combine):
    while len(jax.tree.leaves(pieces)[0]) > 1:
        pieces = jax.vmap(combine)(
            *(jax.tree.map(lambda part: part[side::2], pieces) for side in (0, 1))
        )
    return jax.tree.map(lambda part: part[0], pieces)


def carried_in(shard, axis, combine, identity):
    size, mine = (lax.axis_size(axis), lax.axis_index(axis))
    passed = jnp.arange(size) < mine

    def kept(part, zero, own):
        part = jnp.where(
            passed.reshape(-1, *(1 for _ in own.shape)), part, jnp.asarray(zero, own.dtype)
        )
        return part

    pieces = collected_together(shard, axis)
    return folded_in_pairs(jax.tree.map(kept, pieces, identity, shard), combine)


def gather_turned(arrays, axis, dims):
    turned = [jnp.moveaxis(a, dim, 0) for a, dim in zip(arrays, dims)]
    both = jnp.concatenate([t.reshape(len(t), -1) for t in turned], axis=1)
    filled, at, finished = (lax.all_gather(both, axis, axis=0, tiled=True), 0, [])
    for t, dim in zip(turned, dims):
        share = filled[:, at : at + t[0].size].reshape(-1, *t.shape[1:])
        finished.append(jnp.moveaxis(share, 0, dim))
        at += t[0].size
    return tuple(finished)


def collected_together_2(shard, axis):
    leaves = jax.tree.leaves(shard)
    order = sorted(range(len(leaves)), key=lambda k: -leaves[k].size)
    width = (1, *leaves[order[0]].shape)[-1]
    lines = [
        jnp.pad(leaves[k].reshape(-1), (0, -leaves[k].size % width)).reshape(-1, width)
        for k in order
    ]
    both, at, found = (lax.all_gather(jnp.concatenate(lines), axis), 0, {})
    for k, line in zip(order, lines):
        share = both[:, at : at + len(line)].reshape(len(both), -1)
        found[k] = share[:, : leaves[k].size].reshape(-1, *leaves[k].shape)
        at += len(line)
    numbers = iter(range(len(leaves)))
    return jax.tree.map(lambda _: found[next(numbers)], shard)


def gathered_by_type(shard, axis):
    leaves, found = (jax.tree.leaves(shard), {})
    for leading, a in enumerate(leaves):
        if leading not in found:
            alike = [k for k, b in enumerate(leaves) if b.dtype == a.dtype]
            got = (
                collected_together_2([leaves[k] for k in alike], axis)
                if len(alike) > 1
                else [lax.all_gather(a, axis)]
            )
            for k, b in zip(alike, got):
                found[k] = b
    numbers = iter(range(len(leaves)))
    return jax.tree.map(lambda _: found[next(numbers)], shard)


def carried_in_2(shard, axis, combine, identity):
    size, mine = (lax.axis_size(axis), lax.axis_index(axis))
    everything = gathered_by_type(shard, axis)
    start = jax.tree.map(
        lambda part, zero: jnp.broadcast_to(jnp.asarray(zero, part.dtype), part.shape),
        shard,
        identity,
    )

    def hop(k, before):
        at = size - 1 - k
        reached = at > mine
        new = combine(before, jax.tree.map(lambda part: part[at], everything))
        return jax.tree.map(lambda a, b: jnp.where(reached, a, b), new, before)

    return lax.fori_loop(0, size, hop, start)


def add_pair(earlier, later):
    return (earlier[0] + later[0], earlier[1] + later[1])


def running_states(local_state, local_total):
    shares = in_one_piece((local_state, local_total), "space", 0, 1)
    before = carried_in(
        (shares[0], shares[1]),
        "tm",
        add_pair,
        (jnp.zeros_like(shares[0]), jnp.zeros_like(shares[1])),
    )
    running = add_pair(before, shares)
    return gather_turned((running[0], running[1]), "space", (0, 0))


def later_states(local_state, local_total):
    shares = (sent_and_summed(local_state, "space", 0), sent_and_summed(local_total, "space", 0))
    after = carried_in_2(
        (shares[0], shares[1]),
        "tm",
        add_pair,
        (jnp.zeros_like(shares[0]), jnp.zeros_like(shares[1])),
    )
    running = add_pair(after, shares)
    return gather_turned((running[0], running[1]), "space", (0, 0))


def body(queries, keys_in, values_in, grad_attn):
    row_count = queries.shape[1]
    channels = queries.shape[2]
    heads = channels // HEAD_DIM
    query_rows = queries[0]
    key_rows = keys_in[0]
    value_rows = values_in[0]
    key_pos = jax.nn.relu(key_rows)
    state_part = jnp.einsum(
        "isp,isz->spz",
        key_pos.reshape(row_count, heads, HEAD_DIM),
        value_rows.reshape(row_count, heads, HEAD_DIM),
        preferred_element_type=jnp.float32,
    )
    total_part = jnp.sum(key_pos, axis=0, dtype=jnp.float32)
    state_flat, total_flat = running_states(state_part.reshape(channels, HEAD_DIM), total_part)
    running_state = state_flat.reshape(heads, HEAD_DIM, HEAD_DIM)
    running_total = total_flat.reshape(heads, HEAD_DIM)
    query_position = jax.nn.relu(query_rows).astype(jnp.float32).reshape(row_count, heads, HEAD_DIM)
    numerator = jnp.einsum("igx,gxb->igb", query_position, running_state, precision=HIGH_PRECISION)
    denom = jnp.einsum("rhk,hk->rh", query_position, running_total, precision=HIGH_PRECISION) + 1.0
    attn_f = numerator / denom[..., None]
    mixed = attn_f.reshape(row_count, channels).astype(jnp.bfloat16)
    g_out = grad_attn[0].astype(jnp.float32).reshape(row_count, heads, HEAD_DIM)
    numerator_gradient = g_out / denom[..., None]
    denominator_gradient = -jnp.sum(g_out * attn_f, axis=-1) / denom
    feature_gradient = (
        jnp.einsum("tqd,qwd->tqw", numerator_gradient, running_state, precision=HIGH_PRECISION)
        + denominator_gradient[..., None] * running_total[None]
    )
    grad_queries = jnp.where(
        query_rows.reshape(row_count, heads, HEAD_DIM) > 0, feature_gradient, 0.0
    )
    partial_state_gradient = jnp.einsum(
        "isp,isz->spz", query_position, numerator_gradient, precision=HIGH_PRECISION
    )
    gtotal_part = jnp.einsum(
        "rhk,rh->hk", query_position, denominator_gradient, precision=HIGH_PRECISION
    )
    gstate_flat, gtotal_flat = later_states(
        partial_state_gradient.reshape(channels, HEAD_DIM), gtotal_part.reshape(channels)
    )
    state_gradient = gstate_flat.reshape(heads, HEAD_DIM, HEAD_DIM)
    total_gradient = gtotal_flat.reshape(heads, HEAD_DIM)
    key_wide_float = key_pos.astype(jnp.float32).reshape(row_count, heads, HEAD_DIM)
    value_wide_float = value_rows.astype(jnp.float32).reshape(row_count, heads, HEAD_DIM)
    values_gradient = jnp.einsum(
        "igx,gxb->igb", key_wide_float, state_gradient, precision=HIGH_PRECISION
    )
    key_gradient = (
        jnp.einsum("tqd,qwd->tqw", value_wide_float, state_gradient, precision=HIGH_PRECISION)
        + total_gradient[None]
    )
    grad_keys = jnp.where(key_rows.reshape(row_count, heads, HEAD_DIM) > 0, key_gradient, 0.0)
    return (
        mixed[None],
        grad_queries.reshape(row_count, channels).astype(jnp.bfloat16)[None],
        grad_keys.reshape(row_count, channels).astype(jnp.bfloat16)[None],
        values_gradient.reshape(row_count, channels).astype(jnp.bfloat16)[None],
    )


def solution(mesh):
    placed = (
        P("tm", "space", None),
        P("tm", "space", None),
        P("tm", "space", None),
        P("tm", "space", None),
    )
    return jax.shard_map(
        body,
        mesh=mesh,
        in_specs=placed,
        out_specs=(
            P("tm", "space", None),
            P("tm", "space", None),
            P("tm", "space", None),
            P("tm", "space", None),
        ),
        check_vma=False,
    )
```

profile of v0, /device:TPU:2, one launch (start us, length us, event | category | flops | bytes accessed | tf_op | source)
XLA Modules:
  0.0 212.7 jit_solution(13621507825996979436)
XLA Ops:
  0.6 0.0 copy-start
  0.6 0.0 copy-start.1
  0.7 1.2 convert_reduce_fusion
  1.9 0.3 concatenate.27
  2.2 0.3 fusion.16
  2.6 1.1 pad_maximum_fusion
  3.6 10.2 %all-to-all-start = ((f32[32,35,113]{2,1,0:T(8,128)}), f32[32,35,113]{2,1,0:T(8,128)S(1)}, u32[]{:S(2)}, u32[]{:S(2)}) async-start(f32[32,35,113]{2,1,0:T(8,128)} %pad_maximum_fusion), calls=%async_computation | async-start | bytes 1310720 | tf_op jit(solution)/shard_map/all_to_all | solution.py:19
  13.9 18.0 %all-to-all-done = f32[32,35,113]{2,1,0:T(8,128)S(1)} async-done(((f32[32,35,113]{2,1,0:T(8,128)}), f32[32,35,113]{2,1,0:T(8,128)S(1)}, u32[]{:S(2)}, u32[]{:S(2)}) %all-to-all-start) | async-done | bytes 506272 | tf_op jit(solution)/shard_map/all_to_all | solution.py:19
  31.9 0.1 reduce_sum.46
  32.0 0.2 slice_reduce_fusion.2
  32.2 0.7 broadcast_in_dim.43
  32.9 10.6 %all-to-all-start.1 = ((f32[16,36,112]{2,1,0:T(8,128)}), f32[16,36,112]{2,1,0:T(8,128)S(1)}, u32[]{:S(2)}, u32[]{:S(2)}) async-start(f32[16,36,112]{2,1,0:T(8,128)} %broadcast_in_dim.43), calls=%async_computation.1 | async-start | bytes 655360 | tf_op jit(solution)/shard_map/all_to_all | solution.py:37
  43.5 12.3 %all-to-all-done.1 = f32[16,36,112]{2,1,0:T(8,128)S(1)} async-done(((f32[16,36,112]{2,1,0:T(8,128)}), f32[16,36,112]{2,1,0:T(8,128)S(1)}, u32[]{:S(2)}, u32[]{:S(2)}) %all-to-all-start.1) | async-done | bytes 258080 | tf_op jit(solution)/shard_map/all_to_all | solution.py:37
  55.9 0.1 slice_select_fusion.1
  56.1 0.1 copy.33
  56.2 0.1 slice_add_fusion.4
  56.3 0.1 slice_select_fusion
  56.5 0.1 maximum_bitcast_fusion
  56.6 49.1 %all-gather.1 = f32[32,35,113]{2,1,0:T(8,128)S(1)} all-gather(f32[1,35,113]{2,1,0:T(8,128)S(1)} %maximum_bitcast_fusion), channel_id=1, replica_groups=mesh['tm'=16,'space'=32] {'space'}, dimensions={0}, use_global_device_ids=true | all-gather | bytes 522060 | tf_op jit(solution)/shard_map/all_gather | solution.py:84
  105.7 0.4 slice_reduce_fusion.1
  106.1 0.0 copy-start.3
  106.1 0.1 reshape.155
  106.2 0.3 fusion.17
  106.5 0.5 copy-done.3
  107.0 1.3 fusion.7
  108.4 0.5 fusion.14
  109.0 0.7 all_to_all.18
  109.7 7.1 %all-to-all-start.3 = ((f32[32,1,35]{2,1,0:T(1,128)}), f32[32,1,35]{2,1,0:T(1,128)S(1)}, u32[]{:S(2)}, u32[]{:S(2)}) async-start(f32[32,1,35]{2,1,0:T(1,128)} %all_to_all.18), calls=%async_computation.3 | async-start | bytes 32768 | tf_op jit(solution)/shard_map/all_to_all | solution.py:19
  116.8 0.7 fusion.8
  117.5 0.9 reshape_reshape.8
  118.4 7.2 %all-to-all-done.3 = f32[32,1,35]{2,1,0:T(1,128)S(1)} async-done(((f32[32,1,35]{2,1,0:T(1,128)}), f32[32,1,35]{2,1,0:T(1,128)S(1)}, u32[]{:S(2)}, u32[]{:S(2)}) %all-to-all-start.3) | async-done | bytes 4512 | tf_op jit(solution)/shard_map/all_to_all | solution.py:19
  125.6 5.0 %all-to-all-start.2 = ((f32[32,35,112]{2,1,0:T(8,128)}), f32[32,35,112]{2,1,0:T(8,128)S(1)}, u32[]{:S(2)}, u32[]{:S(2)}) async-start(f32[32,35,112]{2,1,0:T(8,128)} %reshape_reshape.8), calls=%async_computation.2 | async-start | bytes 1310720 | tf_op jit(solution)/shard_map/all_to_all | solution.py:19
  130.5 0.1 broadcast_compare_fusion.1
  130.6 0.1 broadcast_compare_fusion
  130.7 0.1 reshape_reshape.7
  130.8 1.5 fusion.6
  132.3 0.1 reduce_sum.49
  132.4 10.7 %all-to-all-done.2 = f32[32,35,112]{2,1,0:T(8,128)S(1)} async-done(((f32[32,35,112]{2,1,0:T(8,128)}), f32[32,35,112]{2,1,0:T(8,128)S(1)}, u32[]{:S(2)}, u32[]{:S(2)}) %all-to-all-start.2) | async-done | bytes 501792 | tf_op jit(solution)/shard_map/all_to_all | solution.py:19
  143.1 0.1 reduce_sum.48
  143.1 16.0 %all-gather.2 = f32[16,36,112]{2,1,0:T(8,128)S(1)} all-gather(f32[1,36,112]{2,1,0:T(8,128)S(1)} %maximum_bitcast_fusion.1), channel_id=2, replica_groups=mesh['tm'=16,'space'=32] {'tm'}, dimensions={0}, use_global_device_ids=true | all-gather | bytes 274176 | tf_op jit(solution)/shard_map/all_gather | solution.py:100
  159.2 1.1 while.18
  160.3 0.1 copy.35
  160.4 0.1 maximum_bitcast_fusion.2
  160.5 49.2 %all-gather.3 = f32[32,35,113]{2,1,0:T(8,128)S(1)} all-gather(f32[1,35,113]{2,1,0:T(8,128)S(1)} %maximum_bitcast_fusion.2), channel_id=1, replica_groups=mesh['tm'=16,'space'=32] {'space'}, dimensions={0}, use_global_device_ids=true | all-gather | bytes 522060 | tf_op jit(solution)/shard_map/all_gather | solution.py:84
  209.7 0.4 slice_reduce_fusion
  210.1 0.1 add.133
  210.2 1.3 convolution_convert_fusion
  211.6 1.2 fusion.5
  (69 shorter events, 1.0 us)
Async XLA Ops:
  0.6 1.6 copy-start
  0.6 1.2 copy-start.1
  3.6 28.3 %all-to-all-start = ((f32[32,35,113]{2,1,0:T(8,128)}), f32[32,35,113]{2,1,0:T(8,128)S(1)}, u32[]{:S(2)}, u32[]{:S(2)}) async-start(f32[32,35,113]{2,1,0:T(8,128)} %pad_maximum_fusion), calls=%async_computation | async-start | bytes 1310720 | tf_op jit(solution)/shard_map/all_to_all | solution.py:19
  32.9 10.6 %copy-start.2 = (bf16[1,128,1120]{1,2,0:T(8,128)(2,1)S(1)}, bf16[1,128,1120]{1,2,0:T(8,128)(2,1)}, u32[]{:S(2)}) copy-start(bf16[1,128,1120]{1,2,0:T(8,128)(2,1)} %param.6) | copy-start | bytes 860164
  32.9 23.0 %all-to-all-start.1 = ((f32[16,36,112]{2,1,0:T(8,128)}), f32[16,36,112]{2,1,0:T(8,128)S(1)}, u32[]{:S(2)}, u32[]{:S(2)}) async-start(f32[16,36,112]{2,1,0:T(8,128)} %broadcast_in_dim.43), calls=%async_computation.1 | async-start | bytes 655360 | tf_op jit(solution)/shard_map/all_to_all | solution.py:37
  106.1 1.0 copy-start.3
  109.7 15.9 %all-to-all-start.3 = ((f32[32,1,35]{2,1,0:T(1,128)}), f32[32,1,35]{2,1,0:T(1,128)S(1)}, u32[]{:S(2)}, u32[]{:S(2)}) async-start(f32[32,1,35]{2,1,0:T(1,128)} %all_to_all.18), calls=%async_computation.3 | async-start | bytes 32768 | tf_op jit(solution)/shard_map/all_to_all | solution.py:19
  125.6 17.5 %all-to-all-start.2 = ((f32[32,35,112]{2,1,0:T(8,128)}), f32[32,35,112]{2,1,0:T(8,128)S(1)}, u32[]{:S(2)}, u32[]{:S(2)}) async-start(f32[32,35,112]{2,1,0:T(8,128)} %reshape_reshape.8), calls=%async_computation.2 | async-start | bytes 1310720 | tf_op jit(solution)/shard_map/all_to_all | solution.py:19
where the time goes:
time: 213 us
  blocking collectives  114 us (54%)
  waiting for transfers between devices  48.2 us (23%)
  starting transfers between devices  32.8 us (15%)
  matrix products  7.28 us (3%)
  local copies, waits for them, and re-layouts  4.91 us (2%)
  other arithmetic  3.66 us (2%)
    all_gather x2, blocking collectives, gather_turned(): lax.all_gather(both, axis, axis=0, tiled=True)  98.3 us
    all_to_all x3, waiting for transfers between devices, sent_and_summed(): pieces = lax.all_to_all(split_up(shard, dim, size), axis, 0, 0, tiled=True)  35.9 us
    all_to_all x3, starting transfers between devices, sent_and_summed(): pieces = lax.all_to_all(split_up(shard, dim, size), axis, 0, 0, tiled=True)  22.3 us
    all_gather x1, blocking collectives, collected_together_2(): both, at, found = (lax.all_gather(jnp.concatenate(lines), axis), 0, {})  16 us
    all_to_all x1, waiting for transfers between devices, sent_to_all(): lax.all_to_all(jnp.broadcast_to(shard[None], (size, *shard.shape)), axis,...  12.3 us
    all_to_all x1, starting transfers between devices, sent_to_all(): lax.all_to_all(jnp.broadcast_to(shard[None], (size, *shard.shape)), axis,...  10.6 us
  transfers between devices with their start and end apart: 4, of which 4 were waited for; matrix products, arithmetic and copies ran while one was open for 2% of the time, Pallas kernels for 0%

commit v1 on v0

--- a/solution.py
+++ b/solution.py
@@ -81,7 +81,13 @@
 def gather_turned(arrays, axis, dims):
     turned = [jnp.moveaxis(a, dim, 0) for a, dim in zip(arrays, dims)]
     both = jnp.concatenate([t.reshape(len(t), -1) for t in turned], axis=1)
-    filled, at, finished = (lax.all_gather(both, axis, axis=0, tiled=True), 0, [])
+    filled, at, finished = (
+        jnp.concatenate(
+            lax.all_to_all(jnp.stack([both] * lax.axis_size(axis)), axis, 0, 0), axis=0
+        ),
+        0,
+        [],
+    )
     for t, dim in zip(turned, dims):
         share = filled[:, at : at + t[0].size].reshape(-1, *t.shape[1:])
         finished.append(jnp.moveaxis(share, 0, dim))

time: 213 us -> 174 us (0.82)
  the two profiles are of different devices: /device:TPU:2 before, /device:TPU:8 now
where the time goes in v1:
time: 174 us; the launch traced here: 173 us
  waiting for transfers between devices  79.2 us (46%)
  blocking collectives  45.3 us (26%)
  starting transfers between devices  30.6 us (18%)
  matrix products  7.28 us (4%)
  local copies, waits for them, and re-layouts  6.67 us (4%)
  other arithmetic  2.82 us (2%)
    all_to_all x2, waiting for transfers between devices, gather_turned(): lax.all_to_all(jnp.stack([both] * lax.axis_size(axis)), axis, 0, 0)  40.4 us
    all_to_all x1, blocking collectives, sent_and_summed(): pieces = lax.all_to_all(split_up(shard, dim, size), axis, 0, 0, tiled=True)  30.2 us
    all_to_all x2, waiting for transfers between devices, sent_and_summed(): pieces = lax.all_to_all(split_up(shard, dim, size), axis, 0, 0, tiled=True)  26.4 us
    all_gather x1, blocking collectives, collected_together_2(): both, at, found = (lax.all_gather(jnp.concatenate(lines), axis), 0, {})  15.1 us
    all_to_all x1, waiting for transfers between devices, sent_to_all(): lax.all_to_all(jnp.broadcast_to(shard[None], (size, *shard.shape)), axis,...  12.4 us
    all_to_all x1, starting transfers between devices, sent_to_all(): lax.all_to_all(jnp.broadcast_to(shard[None], (size, *shard.shape)), axis,...  10.4 us
    all_to_all x2, starting transfers between devices, sent_and_summed(): pieces = lax.all_to_all(split_up(shard, dim, size), axis, 0, 0, tiled=True)  10.1 us
    all_to_all x2, starting transfers between devices, gather_turned(): lax.all_to_all(jnp.stack([both] * lax.axis_size(axis)), axis, 0, 0)  10.1 us
  transfers between devices with their start and end apart: 5, of which 5 were waited for; matrix products, arithmetic and copies ran while one was open for 2% of the time, Pallas kernels for 0%

profile of v1, /device:TPU:8, one launch (start us, length us, event | category | flops | bytes accessed | tf_op | source)
XLA Modules:
  0.0 173.4 jit_solution(11262973066867783342)
XLA Ops:
  0.7 1.2 convert_reduce_fusion
  1.9 0.3 concatenate.27
  2.2 0.3 fusion.16
  2.6 0.2 pad_maximum_fusion
  2.8 30.2 %all_to_all.34 = f32[32,35,113]{2,1,0:T(8,128)S(1)} all-to-all(f32[32,35,113]{2,1,0:T(8,128)S(1)} %pad_maximum_fusion), channel_id=1, replica_groups=mesh['tm'=16,'space'=32] {'space'}, dimensions={0} | all-to-all | bytes 1012480 | tf_op jit(solution)/shard_map/all_to_all | solution.py:19
  33.0 0.1 reduce_sum.46
  33.1 0.2 slice_reduce_fusion.2
  33.3 0.7 broadcast_in_dim.43
  34.0 10.4 %all-to-all-start.1 = ((f32[16,36,112]{2,1,0:T(8,128)}), f32[16,36,112]{2,1,0:T(8,128)S(1)}, u32[]{:S(2)}, u32[]{:S(2)}) async-start(f32[16,36,112]{2,1,0:T(8,128)} %broadcast_in_dim.43), calls=%async_computation.1 | async-start | bytes 655360 | tf_op jit(solution)/shard_map/all_to_all | solution.py:37
  44.5 12.4 %all-to-all-done.1 = f32[16,36,112]{2,1,0:T(8,128)S(1)} async-done(((f32[16,36,112]{2,1,0:T(8,128)}), f32[16,36,112]{2,1,0:T(8,128)S(1)}, u32[]{:S(2)}, u32[]{:S(2)}) %all-to-all-start.1) | async-done | bytes 258080 | tf_op jit(solution)/shard_map/all_to_all | solution.py:37
  56.9 0.1 slice_select_fusion.1
  57.1 0.1 copy.33
  57.2 0.1 slice_add_fusion.4
  57.3 0.1 slice_select_fusion
  57.5 0.1 pad_maximum_fusion.2
  57.5 0.9 stack.4
  58.4 5.2 %all-to-all-start.2 = ((f32[32,35,113]{2,1,0:T(8,128)}), f32[32,35,113]{2,1,0:T(8,128)S(1)}, u32[]{:S(2)}, u32[]{:S(2)}) async-start(f32[32,35,113]{2,1,0:T(8,128)} %stack.4), calls=%async_computation.2 | async-start | bytes 1310720 | tf_op jit(solution)/shard_map/all_to_all | solution.py:86
  63.6 21.3 %all-to-all-done.2 = f32[32,35,113]{2,1,0:T(8,128)S(1)} async-done(((f32[32,35,113]{2,1,0:T(8,128)}), f32[32,35,113]{2,1,0:T(8,128)S(1)}, u32[]{:S(2)}, u32[]{:S(2)}) %all-to-all-start.2) | async-done | bytes 506272 | tf_op jit(solution)/shard_map/all_to_all | solution.py:86
  85.0 0.4 slice_reduce_fusion.1
  85.4 0.1 reshape.163
  85.5 0.3 fusion.17
  85.8 0.5 copy-done.3
  86.3 1.3 fusion.7
  87.7 0.5 fusion.14
  88.2 0.7 all_to_all.25
  89.0 5.2 %all-to-all-start.4 = ((f32[32,1,35]{2,1,0:T(1,128)}), f32[32,1,35]{2,1,0:T(1,128)S(1)}, u32[]{:S(2)}, u32[]{:S(2)}) async-start(f32[32,1,35]{2,1,0:T(1,128)} %all_to_all.25), calls=%async_computation.4 | async-start | bytes 32768 | tf_op jit(solution)/shard_map/all_to_all | solution.py:19
  94.2 0.7 fusion.8
  94.9 0.9 reshape_reshape.8
  95.8 7.0 %all-to-all-done.4 = f32[32,1,35]{2,1,0:T(1,128)S(1)} async-done(((f32[32,1,35]{2,1,0:T(1,128)}), f32[32,1,35]{2,1,0:T(1,128)S(1)}, u32[]{:S(2)}, u32[]{:S(2)}) %all-to-all-start.4) | async-done | bytes 4512 | tf_op jit(solution)/shard_map/all_to_all | solution.py:19
  102.7 4.9 %all-to-all-start.3 = ((f32[32,35,112]{2,1,0:T(8,128)}), f32[32,35,112]{2,1,0:T(8,128)S(1)}, u32[]{:S(2)}, u32[]{:S(2)}) async-start(f32[32,35,112]{2,1,0:T(8,128)} %reshape_reshape.8), calls=%async_computation.3 | async-start | bytes 1310720 | tf_op jit(solution)/shard_map/all_to_all | solution.py:19
  107.7 0.1 reduce_sum.49
  107.8 19.5 %all-to-all-done.3 = f32[32,35,112]{2,1,0:T(8,128)S(1)} async-done(((f32[32,35,112]{2,1,0:T(8,128)}), f32[32,35,112]{2,1,0:T(8,128)S(1)}, u32[]{:S(2)}, u32[]{:S(2)}) %all-to-all-start.3) | async-done | bytes 501792 | tf_op jit(solution)/shard_map/all_to_all | solution.py:19
  127.2 0.1 reduce_sum.48
  127.3 15.1 %all-gather.1 = f32[16,36,112]{2,1,0:T(8,128)S(1)} all-gather(f32[1,36,112]{2,1,0:T(8,128)S(1)} %maximum_bitcast_fusion), channel_id=2, replica_groups=mesh['tm'=16,'space'=32] {'tm'}, dimensions={0}, use_global_device_ids=true | all-gather | bytes 274176 | tf_op jit(solution)/shard_map/all_gather | solution.py:106
  142.4 1.1 while.18
  143.5 0.1 copy.35
  143.6 0.1 pad_maximum_fusion.3
  143.7 0.9 stack.5
  144.5 4.9 %all-to-all-start.5 = ((f32[32,35,113]{2,1,0:T(8,128)}), f32[32,35,113]{2,1,0:T(8,128)S(1)}, u32[]{:S(2)}, u32[]{:S(2)}) async-start(f32[32,35,113]{2,1,0:T(8,128)} %stack.5), calls=%async_computation.5 | async-start | bytes 1310720 | tf_op jit(solution)/shard_map/all_to_all | solution.py:86
  149.5 0.1 broadcast_compare_fusion.1
  149.6 0.1 broadcast_compare_fusion
  149.7 0.1 reshape_reshape.7
  149.7 1.5 fusion.6
  151.3 19.1 %all-to-all-done.5 = f32[32,35,113]{2,1,0:T(8,128)S(1)} async-done(((f32[32,35,113]{2,1,0:T(8,128)}), f32[32,35,113]{2,1,0:T(8,128)S(1)}, u32[]{:S(2)}, u32[]{:S(2)}) %all-to-all-start.5) | async-done | bytes 506272 | tf_op jit(solution)/shard_map/all_to_all | solution.py:86
  170.4 0.4 slice_reduce_fusion
  170.8 0.1 add.133
  170.9 1.3 convolution_convert_fusion
  172.2 1.2 fusion.5
  (72 shorter events, 1.0 us)
Async XLA Ops:
  0.6 1.6 copy-start
  0.6 1.2 copy-start.1
  34.0 22.8 %all-to-all-start.1 = ((f32[16,36,112]{2,1,0:T(8,128)}), f32[16,36,112]{2,1,0:T(8,128)S(1)}, u32[]{:S(2)}, u32[]{:S(2)}) async-start(f32[16,36,112]{2,1,0:T(8,128)} %broadcast_in_dim.43), calls=%async_computation.1 | async-start | bytes 655360 | tf_op jit(solution)/shard_map/all_to_all | solution.py:37
  58.4 5.2 %copy-start.2 = (bf16[1,128,1120]{1,2,0:T(8,128)(2,1)S(1)}, bf16[1,128,1120]{1,2,0:T(8,128)(2,1)}, u32[]{:S(2)}) copy-start(bf16[1,128,1120]{1,2,0:T(8,128)(2,1)} %param.6) | copy-start | bytes 860164
  58.4 26.5 %all-to-all-start.2 = ((f32[32,35,113]{2,1,0:T(8,128)}), f32[32,35,113]{2,1,0:T(8,128)S(1)}, u32[]{:S(2)}, u32[]{:S(2)}) async-start(f32[32,35,113]{2,1,0:T(8,128)} %stack.4), calls=%async_computation.2 | async-start | bytes 1310720 | tf_op jit(solution)/shard_map/all_to_all | solution.py:86
  85.4 1.0 copy-start.3
  89.0 13.8 %all-to-all-start.4 = ((f32[32,1,35]{2,1,0:T(1,128)}), f32[32,1,35]{2,1,0:T(1,128)S(1)}, u32[]{:S(2)}, u32[]{:S(2)}) async-start(f32[32,1,35]{2,1,0:T(1,128)} %all_to_all.25), calls=%async_computation.4 | async-start | bytes 32768 | tf_op jit(solution)/shard_map/all_to_all | solution.py:19
  102.7 24.5 %all-to-all-start.3 = ((f32[32,35,112]{2,1,0:T(8,128)}), f32[32,35,112]{2,1,0:T(8,128)S(1)}, u32[]{:S(2)}, u32[]{:S(2)}) async-start(f32[32,35,112]{2,1,0:T(8,128)} %reshape_reshape.8), calls=%async_computation.3 | async-start | bytes 1310720 | tf_op jit(solution)/shard_map/all_to_all | solution.py:19
  144.5 25.8 %all-to-all-start.5 = ((f32[32,35,113]{2,1,0:T(8,128)}), f32[32,35,113]{2,1,0:T(8,128)S(1)}, u32[]{:S(2)}, u32[]{:S(2)}) async-start(f32[32,35,113]{2,1,0:T(8,128)} %stack.5), calls=%async_computation.5 | async-start | bytes 1310720 | tf_op jit(solution)/shard_map/all_to_all | solution.py:86
